TPU v7x, 128 devices: a whole 4x4x4 slice. The times are simulated.
128 devices in a mesh: row: 16 (over y_lo, z, core), col: 8 (over x, y_hi).
Axes of the slice: x: 4, y: 4 (y_hi: 2, y_lo: 2; y = y_hi * 2 + y_lo), z: 4, core: 2. Of those that a mesh axis runs over, the one named last changes fastest.
Arguments:
- out_grad: bfloat16 [65536, 256], P(('row', 'col')), may hold values from -6 to 6
- out_bits: int32 [65536, 16], P(('row', 'col')), may hold values from 0 to 65535
- agg_saved: bfloat16 [65536, 256], P(('row', 'col')), may hold values from -6 to 6
- weight: bfloat16 [256, 256], replicated, may hold values from -0.375 to 0.375
- tiles: bfloat16 [16, 8, 512, 128, 128], P('row', 'col'), may hold values from -0.0625 to 0.0625
- tile_coords: int32 [16, 8, 512, 2], P('row', 'col'), may hold values from 0 to 63, as said below
- tile_count: int32 [16, 8], P('row', 'col'), may hold values from 64 to 512, as said below
- in_bits: int32 [65536, 16], P(('row', 'col')), may hold values from 0 to 65535
Outputs:
- weight_grad: float32 [256, 256], replicated
- prev_grad: bfloat16 [65536, 256], P(('row', 'col'))
Inputs may be any that keep to these rules, and one draw needn't show every extreme that they name: `tile_coords`: within one block, all 512 slots name distinct tile positions; tile rows are below 32 and tile columns below 64. `tile_count`: slots at or beyond a block's count are ignored; some block uses all 512 slots.
All inputs are finite; a program needn't handle non-finite values.
Results may differ from a plain program's by a relative error of at most 0.0049.
Values may be sent and summed in bfloat16 or wider, within the bound.
No kernel may reach another device: no remote copies, remote signals or barrier semaphores. Data moves between devices by JAX's collectives and lax.ppermute only.
A program may use at most 128 MiB of HBM per device.

v0:
```python
import math
import jax
import jax.numpy as jnp
from jax import lax
from jax.sharding import PartitionSpec as P

TILE = 128


def unpack(packed):
    shift_list = jnp.arange(16, dtype=jnp.int32)
    bit_values = jnp.right_shift(packed[:, :, None], shift_list[None, None, :]) & 1
    return bit_values.reshape(packed.shape[0], packed.shape[1] * 16)


def total_weight(weight_part, norm_scale):
    return lax.psum(weight_part, ("row", "col")) * norm_scale


def shards(out_grad, out_bits, agg_saved, weight, tiles, tile_coords, tile_count, in_bits):
    row_total = lax.axis_size("row")
    col_total = lax.axis_size("col")
    rows_dev, features = out_grad.shape
    node_total = rows_dev * row_total * col_total
    masked_grad = jnp.where(unpack(out_bits) == 1, out_grad, jnp.zeros_like(out_grad))
    weight_part = lax.dot_general(
        agg_saved, masked_grad, (((0,), (0,)), ((), ())), preferred_element_type=jnp.float32
    )
    hidden_grad = lax.dot_general(
        masked_grad, weight, (((1,), (1,)), ((), ())), preferred_element_type=jnp.float32
    ).astype(jnp.bfloat16)
    gathered = lax.all_gather(hidden_grad, "col", axis=0, tiled=True)
    row_count = gathered.shape[0] // TILE
    row_flat = gathered.reshape(row_count, TILE * features)
    own_tiles = tiles[0, 0]
    own_coords = tile_coords[0, 0]
    tile_total = tile_count[0, 0]
    slot_total = own_tiles.shape[0]
    group_size = min(64, slot_total)
    col_tiles = row_total * rows_dev // TILE
    group_starts = jnp.arange(slot_total // group_size, dtype=jnp.int32) * group_size
    row_ids = jnp.arange(row_count, dtype=jnp.int32)
    norm_scale = 1.0 / math.sqrt(node_total)
    window_ids = jnp.arange(col_tiles, dtype=jnp.int32)

    def scan_group(partial_value, first_slot):
        tile_block = lax.dynamic_slice_in_dim(own_tiles, first_slot, group_size, 0)
        block_coords = lax.dynamic_slice_in_dim(own_coords, first_slot, group_size, 0)
        select = (block_coords[:, 0][:, None] == row_ids[None, :]).astype(jnp.bfloat16)
        picked = jnp.dot(select, row_flat, preferred_element_type=jnp.float32).astype(jnp.bfloat16)
        picked = picked.reshape(group_size, TILE, features)
        products = jnp.einsum(
            "kij,kih->kjh", tile_block, picked, preferred_element_type=jnp.float32
        )
        target = block_coords[:, 1] - 0
        alive_mask = first_slot + jnp.arange(group_size, dtype=jnp.int32) < tile_total
        placing = (window_ids[:, None] == target[None, :]) & alive_mask[None, :]
        placing = placing.astype(jnp.float32)
        added = jnp.dot(
            placing,
            products.reshape(group_size, TILE * features),
            precision=lax.Precision.HIGHEST,
            preferred_element_type=jnp.float32,
        )
        return (partial_value + added, None)

    zero_sums = jnp.zeros((col_tiles, TILE * features), jnp.float32)
    partial_value, unused = lax.scan(scan_group, zero_sums, group_starts)
    flat_sums = partial_value.reshape(col_tiles * TILE, features)
    summed = lax.psum_scatter(flat_sums, "row", scatter_dimension=0, tiled=True)
    weight_grad = total_weight(weight_part, norm_scale)
    prev_grad = jnp.where(unpack(in_bits) == 1, summed, jnp.zeros_like(summed)).astype(jnp.bfloat16)
    return (weight_grad, prev_grad)


def solution(mesh):
    return jax.shard_map(
        shards,
        mesh=mesh,
        in_specs=(
            P(("row", "col"), None),
            P(("row", "col"), None),
            P(("row", "col"), None),
            P(),
            P("row", "col", None, None, None),
            P("row", "col", None, None),
            P("row", "col"),
            P(("row", "col"), None),
        ),
        out_specs=(P(), P(("row", "col"), None)),
        check_vma=False,
    )
```

profile of v0, /device:TPU:0, one launch (start us, length us, event | category | flops | bytes accessed | tf_op | source)
XLA Modules:
  0.0 365.1 jit_solution(10695797896538475142)
XLA Ops:
  8.1 1.1 copy.18
  9.2 0.9 fusion.16
  10.2 1.9 convolution_convert_fusion.1
  12.1 0.9 convolution_bitcast_fusion
  13.2 22.5 %copy.19 = bf16[1,1,512,128,128]{3,4,2,1,0:T(8,128)(2,1)} copy(bf16[1,1,512,128,128]{4,3,2,1,0:T(8,128)(2,1)} %param.14) | data formatting | bytes 33554432 | tf_op args[4]
  35.6 34.1 %all-gather.2.cloned.1.call-done = bf16[4096,256]{1,0:T(8,128)(2,1)} async-done(((bf16[512,256]{1,0:T(8,128)(2,1)}), bf16[4096,256]{1,0:T(8,128)(2,1)}) %all-gather.2.cloned.1.call-update) | async-done | bytes 2097168 | tf_op jit(solution)/shard_map/all_gather | solution.py:32
  69.8 2.9 reshape.32
  72.7 190.7 %while.11 = (s32[]{:T(128)}, f32[64,32768]{1,0:T(8,128)}, s32[8]{0:T(128)S(1)}, s32[512,2]{0,1:T(2,128)}, s32[]{:T(128)}, /*index=5*/bf16[512,128,128]{1,2,0:T(8...) while((s32[]{:T(128)}, f32[64,32768]{1,0:T(8,128)}, s32[8]{0:T(128)S(1)}, ...), condition=%wide.region_2.3_spmd.clone, body=%wide.region_1.2_spmd.clone.sunk | while | flops 2288003072 | bytes 71306032 | solution.py:68
  75.2 1.3 add_compare_fusion.2
  77.3 1.3 convolution_convert_fusion.3
  78.6 1.1 copy.27
  79.7 2.9 fusion.35
  82.5 4.7 %copy.28 = f32[8,8,128,256]{3,1,2,0:T(8,128)S(1)} copy(f32[8,8,128,256]{3,2,1,0:T(8,128)S(1)} %bitcast.55) | data formatting | bytes 16777216 | tf_op jit(solution)/shard_map/while
  87.3 7.4 %convolution_add_fusion.2 = f32[64,32768]{1,0:T(8,128)} fusion(f32[64,32768]{1,0:T(8,128)S(1)} %bitcast.56, f32[64,32768]{1,0:T(8,128)} %get-tuple-element.158, pred[]{:T(512)S(6)} %compare.3, s32[64]{0:T(128)S(1)} %get-tuple-element.146, pred[64]{0:T(512)(128)(4,1)S(1)} %add_compare_fusion.2), kind=kOutput, calls=%fused_computation.2.clone.1 | convolution fusion | flops 1614815232 | bytes 25166144 | tf_op jit(solution)/shard_map/while/body/eval_jaxpr/dot_general | solution.py:59
  97.2 1.3 add_compare_fusion.2
  99.2 1.3 convolution_convert_fusion.3
  100.5 1.1 copy.27
  101.6 2.9 fusion.35
  104.5 4.7 %copy.28 = f32[8,8,128,256]{3,1,2,0:T(8,128)S(1)} copy(f32[8,8,128,256]{3,2,1,0:T(8,128)S(1)} %bitcast.55) | data formatting | bytes 16777216 | tf_op jit(solution)/shard_map/while
  109.2 9.5 %convolution_add_fusion.2 = f32[64,32768]{1,0:T(8,128)} fusion(f32[64,32768]{1,0:T(8,128)S(1)} %bitcast.56, f32[64,32768]{1,0:T(8,128)} %get-tuple-element.158, pred[]{:T(512)S(6)} %compare.3, s32[64]{0:T(128)S(1)} %get-tuple-element.146, pred[64]{0:T(512)(128)(4,1)S(1)} %add_compare_fusion.2), kind=kOutput, calls=%fused_computation.2.clone.1 | convolution fusion | flops 1614815232 | bytes 25166144 | tf_op jit(solution)/shard_map/while/body/eval_jaxpr/dot_general | solution.py:59
  121.3 1.3 add_compare_fusion.2
  123.3 1.3 convolution_convert_fusion.3
  124.6 1.1 copy.27
  125.7 2.9 fusion.35
  128.6 4.7 %copy.28 = f32[8,8,128,256]{3,1,2,0:T(8,128)S(1)} copy(f32[8,8,128,256]{3,2,1,0:T(8,128)S(1)} %bitcast.55) | data formatting | bytes 16777216 | tf_op jit(solution)/shard_map/while
  133.3 9.5 %convolution_add_fusion.2 = f32[64,32768]{1,0:T(8,128)} fusion(f32[64,32768]{1,0:T(8,128)S(1)} %bitcast.56, f32[64,32768]{1,0:T(8,128)} %get-tuple-element.158, pred[]{:T(512)S(6)} %compare.3, s32[64]{0:T(128)S(1)} %get-tuple-element.146, pred[64]{0:T(512)(128)(4,1)S(1)} %add_compare_fusion.2), kind=kOutput, calls=%fused_computation.2.clone.1 | convolution fusion | flops 1614815232 | bytes 25166144 | tf_op jit(solution)/shard_map/while/body/eval_jaxpr/dot_general | solution.py:59
  145.4 1.3 add_compare_fusion.2
  146.7 0.8 constant_dynamic-slice_fusion.2
  147.4 1.3 convolution_convert_fusion.3
  148.7 1.1 copy.27
  149.8 2.9 fusion.35
  152.7 4.7 %copy.28 = f32[8,8,128,256]{3,1,2,0:T(8,128)S(1)} copy(f32[8,8,128,256]{3,2,1,0:T(8,128)S(1)} %bitcast.55) | data formatting | bytes 16777216 | tf_op jit(solution)/shard_map/while
  157.4 9.5 %convolution_add_fusion.2 = f32[64,32768]{1,0:T(8,128)} fusion(f32[64,32768]{1,0:T(8,128)S(1)} %bitcast.56, f32[64,32768]{1,0:T(8,128)} %get-tuple-element.158, pred[]{:T(512)S(6)} %compare.3, s32[64]{0:T(128)S(1)} %get-tuple-element.146, pred[64]{0:T(512)(128)(4,1)S(1)} %add_compare_fusion.2), kind=kOutput, calls=%fused_computation.2.clone.1 | convolution fusion | flops 1614815232 | bytes 25166144 | tf_op jit(solution)/shard_map/while/body/eval_jaxpr/dot_general | solution.py:59
  169.5 1.3 add_compare_fusion.2
  171.6 1.3 convolution_convert_fusion.3
  172.8 1.1 copy.27
  174.0 2.9 fusion.35
  176.8 4.7 %copy.28 = f32[8,8,128,256]{3,1,2,0:T(8,128)S(1)} copy(f32[8,8,128,256]{3,2,1,0:T(8,128)S(1)} %bitcast.55) | data formatting | bytes 16777216 | tf_op jit(solution)/shard_map/while
  181.6 9.5 %convolution_add_fusion.2 = f32[64,32768]{1,0:T(8,128)} fusion(f32[64,32768]{1,0:T(8,128)S(1)} %bitcast.56, f32[64,32768]{1,0:T(8,128)} %get-tuple-element.158, pred[]{:T(512)S(6)} %compare.3, s32[64]{0:T(128)S(1)} %get-tuple-element.146, pred[64]{0:T(512)(128)(4,1)S(1)} %add_compare_fusion.2), kind=kOutput, calls=%fused_computation.2.clone.1 | convolution fusion | flops 1614815232 | bytes 25166144 | tf_op jit(solution)/shard_map/while/body/eval_jaxpr/dot_general | solution.py:59
  193.6 1.3 add_compare_fusion.2
  195.7 1.3 convolution_convert_fusion.3
  197.0 1.1 copy.27
  198.1 2.9 fusion.35
  200.9 4.7 %copy.28 = f32[8,8,128,256]{3,1,2,0:T(8,128)S(1)} copy(f32[8,8,128,256]{3,2,1,0:T(8,128)S(1)} %bitcast.55) | data formatting | bytes 16777216 | tf_op jit(solution)/shard_map/while
  205.7 9.5 %convolution_add_fusion.2 = f32[64,32768]{1,0:T(8,128)} fusion(f32[64,32768]{1,0:T(8,128)S(1)} %bitcast.56, f32[64,32768]{1,0:T(8,128)} %get-tuple-element.158, pred[]{:T(512)S(6)} %compare.3, s32[64]{0:T(128)S(1)} %get-tuple-element.146, pred[64]{0:T(512)(128)(4,1)S(1)} %add_compare_fusion.2), kind=kOutput, calls=%fused_computation.2.clone.1 | convolution fusion | flops 1614815232 | bytes 25166144 | tf_op jit(solution)/shard_map/while/body/eval_jaxpr/dot_general | solution.py:59
  217.7 1.3 add_compare_fusion.2
  219.8 1.3 convolution_convert_fusion.3
  221.1 1.1 copy.27
  222.2 2.9 fusion.35
  225.0 4.7 %copy.28 = f32[8,8,128,256]{3,1,2,0:T(8,128)S(1)} copy(f32[8,8,128,256]{3,2,1,0:T(8,128)S(1)} %bitcast.55) | data formatting | bytes 16777216 | tf_op jit(solution)/shard_map/while
  229.8 9.5 %convolution_add_fusion.2 = f32[64,32768]{1,0:T(8,128)} fusion(f32[64,32768]{1,0:T(8,128)S(1)} %bitcast.56, f32[64,32768]{1,0:T(8,128)} %get-tuple-element.158, pred[]{:T(512)S(6)} %compare.3, s32[64]{0:T(128)S(1)} %get-tuple-element.146, pred[64]{0:T(512)(128)(4,1)S(1)} %add_compare_fusion.2), kind=kOutput, calls=%fused_computation.2.clone.1 | convolution fusion | flops 1614815232 | bytes 25166144 | tf_op jit(solution)/shard_map/while/body/eval_jaxpr/dot_general | solution.py:59
  241.8 1.3 add_compare_fusion.2
  243.9 1.3 convolution_convert_fusion.3
  245.2 1.1 copy.27
  246.3 2.9 fusion.35
  249.1 4.7 %copy.28 = f32[8,8,128,256]{3,1,2,0:T(8,128)S(1)} copy(f32[8,8,128,256]{3,2,1,0:T(8,128)S(1)} %bitcast.55) | data formatting | bytes 16777216 | tf_op jit(solution)/shard_map/while
  253.9 9.5 %convolution_add_fusion.2 = f32[64,32768]{1,0:T(8,128)} fusion(f32[64,32768]{1,0:T(8,128)S(1)} %bitcast.56, f32[64,32768]{1,0:T(8,128)} %get-tuple-element.158, pred[]{:T(512)S(6)} %compare.3, s32[64]{0:T(128)S(1)} %get-tuple-element.146, pred[64]{0:T(512)(128)(4,1)S(1)} %add_compare_fusion.2), kind=kOutput, calls=%fused_computation.2.clone.1 | convolution fusion | flops 1614815232 | bytes 25166144 | tf_op jit(solution)/shard_map/while/body/eval_jaxpr/dot_general | solution.py:59
  263.4 9.2 %reshape.33 = f32[8192,256]{1,0:T(8,128)} reshape(f32[64,32768]{1,0:T(8,128)} %get-tuple-element.49) | data formatting | bytes 16777216 | tf_op jit(solution)/shard_map/reshape | solution.py:69
  272.6 8.9 %copy.20 = f32[8192,256]{0,1:T(8,128)} copy(f32[8192,256]{1,0:T(8,128)} %reshape.33) | data formatting | bytes 16777216 | tf_op jit(solution)/shard_map/reshape | solution.py:69
  281.6 1.0 broadcast_multiply_fusion
  282.6 0.8 copy.21
  283.5 72.1 %reduce-scatter.2.cloned.1.call-done = f32[512,256]{0,1:T(8,128)} async-done(((f32[8192,256]{0,1:T(8,128)}), f32[512,256]{0,1:T(8,128)}) %reduce-scatter.2.cloned.1.call-update) | async-done | bytes 524304 | tf_op jit(solution)/shard_map/reduce_scatter | solution.py:70
  355.6 1.2 select_convert_fusion
  356.8 0.8 copy.22
  (40 shorter events, 10.4 us)
Async XLA Ops:
  8.0 4.1 %copy-start = (bf16[512,256]{1,0:T(8,128)(2,1)S(1)}, bf16[512,256]{1,0:T(8,128)(2,1)}, u32[]{:S(2)}) copy-start(bf16[512,256]{1,0:T(8,128)(2,1)} %param.12) | copy-start | bytes 786436
  8.0 61.8 %all-gather.2.cloned.1.call-start = ((), (), s32[]{:S(2)}) async-start(), calls=%async_computation.2 | async-start | bytes 2359296 | tf_op jit(solution)/shard_map/all_gather | solution.py:32
  12.1 269.6 %all-reduce.2.cloned.1.call-start = ((), (), s32[]{:S(2)}) async-start(), calls=%async_computation.1 | async-start | bytes 524288 | tf_op jit(solution)/shard_map/psum | solution.py:17
  13.1 342.5 %reduce-scatter.2.cloned.1.call-start = ((), (), s32[]{:S(2)}) async-start(), calls=%async_computation.3 | async-start | bytes 8912896 | tf_op jit(solution)/shard_map/reduce_scatter | solution.py:70
  272.6 85.0 %copy-start.1 = (bf16[512,256]{1,0:T(8,128)(2,1)S(1)}, bf16[512,256]{1,0:T(8,128)(2,1)}, u32[]{:S(2)}) copy-start(bf16[512,256]{1,0:T(8,128)(2,1)} %param.12) | copy-start | bytes 786436
  281.6 74.0 %copy-start.2 = (s32[512,16]{0,1:T(8,128)S(1)}, s32[512,16]{0,1:T(8,128)}, u32[]{:S(2)}) copy-start(s32[512,16]{0,1:T(8,128)} %param.17) | copy-start | bytes 98308
Sparse Core Ops, SparseCore 0:
  12.2 57.5 all-gather.1
  281.7 73.8 reduce-scatter.1
Sparse Core Ops, SparseCore 1:
  17.9 154.3 all-reduce.1
where the time goes:
time: 367 us; the launch traced here: 365 us
  matrix products  110 us (30%)
  waiting for transfers between devices  106 us (29%)
  local copies, waits for them, and re-layouts  104 us (28%)
  loops' own time  15.8 us (4%)
  between operations  15.6 us (4%)
  other arithmetic  13.5 us (4%)
    dot_general x8, matrix products, scan_group(): jnp.dot(placing, products.reshape(group_size, TILE * features), precision...  73.9 us
    reduce_scatter x1, waiting for transfers between devices, shards(): summed = lax.psum_scatter(flat_sums, 'row', scatter_dimension=0, tiled=True)  72.1 us
    while x16, local copies, waits for them, and re-layouts  46.7 us
    all_gather x1, waiting for transfers between devices, shards(): gathered = lax.all_gather(hidden_grad, 'col', axis=0, tiled=True)  34.1 us
    unnamed x10, local copies, waits for them, and re-layouts  25.2 us
    dot_general x8, matrix products, scan_group(): jnp.einsum('kij,kih->kjh', tile_block, picked, preferred_element_type=jnp...  22.8 us
    reshape x2, local copies, waits for them, and re-layouts, shards(): flat_sums = partial_value.reshape(col_tiles * TILE, features)  18.2 us
    another operation x1, loops' own time, shards(): partial_value, unused = lax.scan(scan_group, zero_sums, group_starts)  15.8 us
  transfers between devices with their start and end apart: 3, of which 2 were waited for; matrix products, arithmetic and copies ran while one was open for 61% of the time, Pallas kernels for 0%

commit v1 on v0

--- a/solution.py
+++ b/solution.py
@@ -29,7 +29,9 @@
     hidden_grad = lax.dot_general(
         masked_grad, weight, (((1,), (1,)), ((), ())), preferred_element_type=jnp.float32
     ).astype(jnp.bfloat16)
-    gathered = lax.all_gather(hidden_grad, "col", axis=0, tiled=True)
+    gathered = jnp.concatenate(
+        lax.all_to_all(jnp.stack([hidden_grad] * lax.axis_size("col")), "col", 0, 0), axis=0
+    )
     row_count = gathered.shape[0] // TILE
     row_flat = gathered.reshape(row_count, TILE * features)
     own_tiles = tiles[0, 0]

time: 367 us -> 348 us (0.948)
  waiting for transfers between devices: 106 us -> 79.5 us
  starting transfers between devices: 0.12 us -> 7.09 us
    all_gather x1 -> x0, waiting for transfers between devices: 34.1 us -> none  [shards(): gathered = lax.all_gather(hidden_grad, 'col', axis=0, tiled=True)]
    all_to_all x0 -> x1, waiting for transfers between devices: none -> 8.16 us  [shards(): lax.all_to_all(jnp.stack([hidden_grad] * lax.axis_size('col')), 'col', 0, 0)]
    all_to_all x0 -> x1, starting transfers between devices: none -> 7.01 us  [shards(): lax.all_to_all(jnp.stack([hidden_grad] * lax.axis_size('col')), 'col', 0, 0)]
    another operation x0 -> x2, local copies, waits for them, and re-layouts: none -> 4.34 us  [the longest x1 2.88 us: shards(): row_flat = gathered.reshape(row_count, TILE * features)]
  transfers between devices with their start and end apart: 3 -> 3, of which waited for: 2 -> 2; matrix products, arithmetic and copies ran while one was open for 61% -> 64% of each run, Pallas kernels for 0% -> 0%
where the time goes in v1:
time: 348 us; the launch traced here: 345 us
  matrix products  109 us (31%)
  local copies, waits for them, and re-layouts  106 us (30%)
  waiting for transfers between devices  79.5 us (23%)
  between operations  15.6 us (4%)
  loops' own time  15.2 us (4%)
  other arithmetic  13.3 us (4%)
  starting transfers between devices  7.09 us (2%)
    dot_general x8, matrix products, scan_group(): jnp.dot(placing, products.reshape(group_size, TILE * features), precision...  73.7 us
    reduce_scatter x1, waiting for transfers between devices, shards(): summed = lax.psum_scatter(flat_sums, 'row', scatter_dimension=0, tiled=True)  71.3 us
    while x16, local copies, waits for them, and re-layouts  46.7 us
    unnamed x10, local copies, waits for them, and re-layouts  25.1 us
    dot_general x8, matrix products, scan_group(): jnp.einsum('kij,kih->kjh', tile_block, picked, preferred_element_type=jnp...  22.9 us
    reshape x2, local copies, waits for them, and re-layouts, shards(): flat_sums = partial_value.reshape(col_tiles * TILE, features)  18.2 us
    another operation x1, loops' own time, shards(): partial_value, unused = lax.scan(scan_group, zero_sums, group_starts)  15.2 us
    dot_general x8, matrix products, scan_group(): jnp.dot(select, row_flat, preferred_element_type=jnp.float32)  10.3 us
  transfers between devices with their start and end apart: 3, of which 2 were waited for; matrix products, arithmetic and copies ran while one was open for 64% of the time, Pallas kernels for 0%

profile of v1, /device:TPU:0, one launch (start us, length us, event | category | flops | bytes accessed | tf_op | source)
XLA Modules:
  0.0 345.4 jit_solution(10893591865266954260)
XLA Ops:
  8.1 1.1 copy.18
  9.2 0.9 fusion.16
  10.1 1.2 convolution_convert_fusion.1
  11.3 1.5 stack.2
  12.8 7.0 %all-to-all-start = ((bf16[8,512,256]{2,1,0:T(8,128)(2,1)}), bf16[8,512,256]{2,1,0:T(8,128)(2,1)}, u32[]{:S(2)}, u32[]{:S(2)}) async-start(bf16[8,512,256]{2,1,0:T(8,128)(2,1)} %stack.2), calls=%async_computation | async-start | bytes 4194304 | tf_op jit(solution)/shard_map/all_to_all | solution.py:33
  19.8 0.9 convolution_bitcast_fusion
  20.9 22.3 %copy.19 = bf16[1,1,512,128,128]{3,4,2,1,0:T(8,128)(2,1)} copy(bf16[1,1,512,128,128]{4,3,2,1,0:T(8,128)(2,1)} %param.14) | data formatting | bytes 33554432 | tf_op args[4]
  43.2 8.2 %all-to-all-done = bf16[8,512,256]{2,1,0:T(8,128)(2,1)} async-done(((bf16[8,512,256]{2,1,0:T(8,128)(2,1)}), bf16[8,512,256]{2,1,0:T(8,128)(2,1)}, u32[]{:S(2)}, u32[]{:S(2)}) %all-to-all-start) | async-done | bytes 2097184 | tf_op jit(solution)/shard_map/all_to_all | solution.py:33
  51.4 2.9 reshape_reshape.3
  54.3 190.3 %while.11 = (s32[]{:T(128)}, f32[64,32768]{1,0:T(8,128)}, s32[8]{0:T(128)S(1)}, s32[512,2]{0,1:T(2,128)}, s32[]{:T(128)}, /*index=5*/bf16[512,128,128]{1,2,0:T(8...) while((s32[]{:T(128)}, f32[64,32768]{1,0:T(8,128)}, s32[8]{0:T(128)S(1)}, ...), condition=%wide.region_2.3_spmd.clone, body=%wide.region_1.2_spmd.clone.sunk | while | flops 2288003072 | bytes 71306032 | solution.py:70
  56.8 1.3 add_compare_fusion.2
  58.8 1.3 convolution_convert_fusion.3
  60.1 1.1 copy.27
  61.2 2.9 fusion.35
  64.1 4.7 %copy.28 = f32[8,8,128,256]{3,1,2,0:T(8,128)S(1)} copy(f32[8,8,128,256]{3,2,1,0:T(8,128)S(1)} %bitcast.55) | data formatting | bytes 16777216 | tf_op jit(solution)/shard_map/while
  68.9 7.3 %convolution_add_fusion.2 = f32[64,32768]{1,0:T(8,128)} fusion(f32[64,32768]{1,0:T(8,128)S(1)} %bitcast.56, f32[64,32768]{1,0:T(8,128)} %get-tuple-element.158, pred[]{:T(512)S(6)} %compare.3, s32[64]{0:T(128)S(1)} %get-tuple-element.146, pred[64]{0:T(512)(128)(4,1)S(1)} %add_compare_fusion.2), kind=kOutput, calls=%fused_computation.2.clone.1 | convolution fusion | flops 1614815232 | bytes 25166144 | tf_op jit(solution)/shard_map/while/body/eval_jaxpr/dot_general | solution.py:61
  78.7 1.3 add_compare_fusion.2
  80.7 1.3 convolution_convert_fusion.3
  82.0 1.1 copy.27
  83.1 2.9 fusion.35
  86.0 4.7 %copy.28 = f32[8,8,128,256]{3,1,2,0:T(8,128)S(1)} copy(f32[8,8,128,256]{3,2,1,0:T(8,128)S(1)} %bitcast.55) | data formatting | bytes 16777216 | tf_op jit(solution)/shard_map/while
  90.8 9.5 %convolution_add_fusion.2 = f32[64,32768]{1,0:T(8,128)} fusion(f32[64,32768]{1,0:T(8,128)S(1)} %bitcast.56, f32[64,32768]{1,0:T(8,128)} %get-tuple-element.158, pred[]{:T(512)S(6)} %compare.3, s32[64]{0:T(128)S(1)} %get-tuple-element.146, pred[64]{0:T(512)(128)(4,1)S(1)} %add_compare_fusion.2), kind=kOutput, calls=%fused_computation.2.clone.1 | convolution fusion | flops 1614815232 | bytes 25166144 | tf_op jit(solution)/shard_map/while/body/eval_jaxpr/dot_general | solution.py:61
  102.8 1.3 add_compare_fusion.2
  104.8 1.3 convolution_convert_fusion.3
  106.1 1.1 copy.27
  107.2 2.9 fusion.35
  110.1 4.7 %copy.28 = f32[8,8,128,256]{3,1,2,0:T(8,128)S(1)} copy(f32[8,8,128,256]{3,2,1,0:T(8,128)S(1)} %bitcast.55) | data formatting | bytes 16777216 | tf_op jit(solution)/shard_map/while
  114.8 9.5 %convolution_add_fusion.2 = f32[64,32768]{1,0:T(8,128)} fusion(f32[64,32768]{1,0:T(8,128)S(1)} %bitcast.56, f32[64,32768]{1,0:T(8,128)} %get-tuple-element.158, pred[]{:T(512)S(6)} %compare.3, s32[64]{0:T(128)S(1)} %get-tuple-element.146, pred[64]{0:T(512)(128)(4,1)S(1)} %add_compare_fusion.2), kind=kOutput, calls=%fused_computation.2.clone.1 | convolution fusion | flops 1614815232 | bytes 25166144 | tf_op jit(solution)/shard_map/while/body/eval_jaxpr/dot_general | solution.py:61
  126.8 1.3 add_compare_fusion.2
  128.8 1.3 convolution_convert_fusion.3
  130.1 1.1 copy.27
  131.2 2.9 fusion.35
  134.1 4.7 %copy.28 = f32[8,8,128,256]{3,1,2,0:T(8,128)S(1)} copy(f32[8,8,128,256]{3,2,1,0:T(8,128)S(1)} %bitcast.55) | data formatting | bytes 16777216 | tf_op jit(solution)/shard_map/while
  138.9 9.5 %convolution_add_fusion.2 = f32[64,32768]{1,0:T(8,128)} fusion(f32[64,32768]{1,0:T(8,128)S(1)} %bitcast.56, f32[64,32768]{1,0:T(8,128)} %get-tuple-element.158, pred[]{:T(512)S(6)} %compare.3, s32[64]{0:T(128)S(1)} %get-tuple-element.146, pred[64]{0:T(512)(128)(4,1)S(1)} %add_compare_fusion.2), kind=kOutput, calls=%fused_computation.2.clone.1 | convolution fusion | flops 1614815232 | bytes 25166144 | tf_op jit(solution)/shard_map/while/body/eval_jaxpr/dot_general | solution.py:61
  150.9 1.3 add_compare_fusion.2
  152.9 1.3 convolution_convert_fusion.3
  154.2 1.1 copy.27
  155.3 2.9 fusion.35
  158.2 4.7 %copy.28 = f32[8,8,128,256]{3,1,2,0:T(8,128)S(1)} copy(f32[8,8,128,256]{3,2,1,0:T(8,128)S(1)} %bitcast.55) | data formatting | bytes 16777216 | tf_op jit(solution)/shard_map/while
  162.9 9.5 %convolution_add_fusion.2 = f32[64,32768]{1,0:T(8,128)} fusion(f32[64,32768]{1,0:T(8,128)S(1)} %bitcast.56, f32[64,32768]{1,0:T(8,128)} %get-tuple-element.158, pred[]{:T(512)S(6)} %compare.3, s32[64]{0:T(128)S(1)} %get-tuple-element.146, pred[64]{0:T(512)(128)(4,1)S(1)} %add_compare_fusion.2), kind=kOutput, calls=%fused_computation.2.clone.1 | convolution fusion | flops 1614815232 | bytes 25166144 | tf_op jit(solution)/shard_map/while/body/eval_jaxpr/dot_general | solution.py:61
  174.9 1.3 add_compare_fusion.2
  177.0 1.3 convolution_convert_fusion.3
  178.3 1.1 copy.27
  179.4 2.9 fusion.35
  182.2 4.7 %copy.28 = f32[8,8,128,256]{3,1,2,0:T(8,128)S(1)} copy(f32[8,8,128,256]{3,2,1,0:T(8,128)S(1)} %bitcast.55) | data formatting | bytes 16777216 | tf_op jit(solution)/shard_map/while
  187.0 9.5 %convolution_add_fusion.2 = f32[64,32768]{1,0:T(8,128)} fusion(f32[64,32768]{1,0:T(8,128)S(1)} %bitcast.56, f32[64,32768]{1,0:T(8,128)} %get-tuple-element.158, pred[]{:T(512)S(6)} %compare.3, s32[64]{0:T(128)S(1)} %get-tuple-element.146, pred[64]{0:T(512)(128)(4,1)S(1)} %add_compare_fusion.2), kind=kOutput, calls=%fused_computation.2.clone.1 | convolution fusion | flops 1614815232 | bytes 25166144 | tf_op jit(solution)/shard_map/while/body/eval_jaxpr/dot_general | solution.py:61
  199.0 1.3 add_compare_fusion.2
  201.0 1.3 convolution_convert_fusion.3
  202.3 1.1 copy.27
  203.4 2.9 fusion.35
  206.3 4.7 %copy.28 = f32[8,8,128,256]{3,1,2,0:T(8,128)S(1)} copy(f32[8,8,128,256]{3,2,1,0:T(8,128)S(1)} %bitcast.55) | data formatting | bytes 16777216 | tf_op jit(solution)/shard_map/while
  211.0 9.5 %convolution_add_fusion.2 = f32[64,32768]{1,0:T(8,128)} fusion(f32[64,32768]{1,0:T(8,128)S(1)} %bitcast.56, f32[64,32768]{1,0:T(8,128)} %get-tuple-element.158, pred[]{:T(512)S(6)} %compare.3, s32[64]{0:T(128)S(1)} %get-tuple-element.146, pred[64]{0:T(512)(128)(4,1)S(1)} %add_compare_fusion.2), kind=kOutput, calls=%fused_computation.2.clone.1 | convolution fusion | flops 1614815232 | bytes 25166144 | tf_op jit(solution)/shard_map/while/body/eval_jaxpr/dot_general | solution.py:61
  223.0 1.3 add_compare_fusion.2
  225.1 1.3 convolution_convert_fusion.3
  226.4 1.1 copy.27
  227.5 2.9 fusion.35
  230.3 4.7 %copy.28 = f32[8,8,128,256]{3,1,2,0:T(8,128)S(1)} copy(f32[8,8,128,256]{3,2,1,0:T(8,128)S(1)} %bitcast.55) | data formatting | bytes 16777216 | tf_op jit(solution)/shard_map/while
  235.1 9.5 %convolution_add_fusion.2 = f32[64,32768]{1,0:T(8,128)} fusion(f32[64,32768]{1,0:T(8,128)S(1)} %bitcast.56, f32[64,32768]{1,0:T(8,128)} %get-tuple-element.158, pred[]{:T(512)S(6)} %compare.3, s32[64]{0:T(128)S(1)} %get-tuple-element.146, pred[64]{0:T(512)(128)(4,1)S(1)} %add_compare_fusion.2), kind=kOutput, calls=%fused_computation.2.clone.1 | convolution fusion | flops 1614815232 | bytes 25166144 | tf_op jit(solution)/shard_map/while/body/eval_jaxpr/dot_general | solution.py:61
  244.5 9.2 %reshape.31 = f32[8192,256]{1,0:T(8,128)} reshape(f32[64,32768]{1,0:T(8,128)} %get-tuple-element.49) | data formatting | bytes 16777216 | tf_op jit(solution)/shard_map/reshape | solution.py:71
  253.8 9.0 %copy.20 = f32[8192,256]{0,1:T(8,128)} copy(f32[8192,256]{1,0:T(8,128)} %reshape.31) | data formatting | bytes 16777216 | tf_op jit(solution)/shard_map/reshape | solution.py:71
  262.8 1.0 broadcast_multiply_fusion
  264.6 71.3 %reduce-scatter.2.cloned.1.call-done = f32[512,256]{0,1:T(8,128)} async-done(((f32[8192,256]{0,1:T(8,128)}), f32[512,256]{0,1:T(8,128)}) %reduce-scatter.2.cloned.1.call-update) | async-done | bytes 524304 | tf_op jit(solution)/shard_map/reduce_scatter | solution.py:72
  336.0 1.2 select_convert_fusion
  337.1 0.8 copy.22
  (40 shorter events, 12.3 us)
Async XLA Ops:
  8.0 11.8 %copy-start = (bf16[512,256]{1,0:T(8,128)(2,1)S(1)}, bf16[512,256]{1,0:T(8,128)(2,1)}, u32[]{:S(2)}) copy-start(bf16[512,256]{1,0:T(8,128)(2,1)} %param.12) | copy-start | bytes 786436
  12.8 38.6 %all-to-all-start = ((bf16[8,512,256]{2,1,0:T(8,128)(2,1)}), bf16[8,512,256]{2,1,0:T(8,128)(2,1)}, u32[]{:S(2)}, u32[]{:S(2)}) async-start(bf16[8,512,256]{2,1,0:T(8,128)(2,1)} %stack.2), calls=%async_computation | async-start | bytes 4194304 | tf_op jit(solution)/shard_map/all_to_all | solution.py:33
  19.8 243.0 %all-reduce.2.cloned.1.call-start = ((), (), s32[]{:S(2)}) async-start(), calls=%async_computation.2 | async-start | bytes 524288 | tf_op jit(solution)/shard_map/psum | solution.py:17
  20.8 315.2 %reduce-scatter.2.cloned.1.call-start = ((), (), s32[]{:S(2)}) async-start(), calls=%async_computation.3 | async-start | bytes 8912896 | tf_op jit(solution)/shard_map/reduce_scatter | solution.py:72
  253.8 84.2 %copy-start.1 = (bf16[512,256]{1,0:T(8,128)(2,1)S(1)}, bf16[512,256]{1,0:T(8,128)(2,1)}, u32[]{:S(2)}) copy-start(bf16[512,256]{1,0:T(8,128)(2,1)} %param.12) | copy-start | bytes 786436
  262.8 73.2 %copy-start.2 = (s32[512,16]{0,1:T(8,128)S(1)}, s32[512,16]{0,1:T(8,128)}, u32[]{:S(2)}) copy-start(s32[512,16]{0,1:T(8,128)} %param.17) | copy-start | bytes 98308
Sparse Core Ops, SparseCore 0:
  25.9 150.8 all-reduce.1
Sparse Core Ops, SparseCore 1:
  262.9 73.0 reduce-scatter.1
